TPU v7x, 32 devices: a whole 2x2x4 slice. The times are simulated.
32 devices in a mesh: groups: 2 (over x), tok: 16 (over z, y, core).
Axes of the slice: x: 2, y: 2, z: 4, core: 2. Of those that a mesh axis runs over, the one named last changes fastest.
Arguments:
- queries: bfloat16 [1024, 1024], P('tok'), may hold values from -64 to 64
- tokens: bfloat16 [32768, 1024], P(('groups', 'tok')), parts along dimension 0, may hold values from -6 to 6
- key_weight: bfloat16 [1024, 1024], replicated, may hold values from -1 to 1
- value_weight: bfloat16 [1024, 1024], replicated, may hold values from -0.1875 to 0.1875
- out_weight: bfloat16 [1024, 1024], replicated, may hold values from -0.1875 to 0.1875
Outputs:
- latent_update: bfloat16 [2048, 1024], P(('groups', 'tok')), parts along dimension 0
There are 2 independent parts, one for each index of `groups`. A program takes and returns all parts, laid end to end along the dimension named above; an argument that names none is the same for every part. Nothing has to cross between parts.
All inputs are finite; a program needn't handle non-finite values.
Results may differ from a plain program's by a relative error of at most 0.0075.
The roundings to bfloat16 on the way count: a program that leaves them out, or rounds other values in their place, can miss the bound.
Values may be sent and summed in bfloat16 or wider, within the bound.
A program may use at most 64 MiB of HBM per device.

v0:
```python
import jax
import jax.numpy as jnp
from jax import lax
from jax.sharding import PartitionSpec as P

H = 16
HD = 64


epsilon = 1e-05


def layer_norm(matrix):
    widened = matrix.astype(jnp.float32)
    center = widened - jnp.mean(widened, axis=1, keepdims=True)
    spread = jnp.mean(center * center, axis=1, keepdims=True)
    return (center * lax.rsqrt(spread + epsilon)).astype(jnp.bfloat16)


def head_partials(gathered, key_rows, value_rows, head_index):
    first_col = head_index * HD
    head_query = lax.dynamic_slice_in_dim(gathered, first_col, HD, 1)
    head_keys = lax.dynamic_slice_in_dim(key_rows, first_col, HD, 1)
    head_values = lax.dynamic_slice_in_dim(value_rows, first_col, HD, 1)
    scores = lax.dot_general(
        head_query, head_keys, (((1,), (1,)), ((), ())), preferred_element_type=jnp.float32
    ) * HD ** (-0.5)
    row_max = jnp.max(scores, axis=1)
    weights = jnp.exp(scores - row_max[:, None])
    totals = jnp.sum(weights, axis=1)
    partial_value = jnp.dot(
        weights.astype(jnp.bfloat16), head_values, preferred_element_type=jnp.float32
    )
    return (row_max, totals, partial_value)


def on_device(queries, tokens, key_weight, value_weight, out_weight):
    tok_count = lax.axis_size("tok")
    gathered = lax.all_gather(queries, "tok", axis=0, tiled=True)
    normed = layer_norm(tokens)
    key_rows = jnp.dot(normed, key_weight, preferred_element_type=jnp.float32).astype(jnp.bfloat16)
    value_rows = jnp.dot(normed, value_weight, preferred_element_type=jnp.float32).astype(
        jnp.bfloat16
    )

    def one_head(head_index):
        return head_partials(gathered, key_rows, value_rows, head_index)

    head_max, head_total, head_out = lax.map(one_head, jnp.arange(H, dtype=jnp.int32))
    latent_count = gathered.shape[0]
    owned_rows = latent_count // tok_count
    row_max = jnp.transpose(head_max)
    totals = jnp.transpose(head_total)
    partial_value = jnp.transpose(head_out, (1, 0, 2)).reshape(latent_count, H * HD)
    global_max = lax.pmax(row_max.astype(jnp.bfloat16), "tok").astype(row_max.dtype)
    factor = jnp.exp(row_max - global_max)
    scaled_out = (partial_value.reshape(latent_count, H, HD) * factor[..., None]).reshape(
        latent_count, H * HD
    )
    summed_out, summed_total = (
        lax.psum_scatter(scaled_out, "tok", scatter_dimension=0, tiled=True),
        lax.psum_scatter(totals * factor, "tok", scatter_dimension=0, tiled=True),
    )
    summed_out = summed_out.reshape(owned_rows, H, HD)
    attended = (
        (summed_out / summed_total[..., None]).reshape(owned_rows, H * HD).astype(jnp.bfloat16)
    )
    return jnp.dot(attended, out_weight, preferred_element_type=jnp.float32).astype(jnp.bfloat16)


def solution(mesh):
    placed = (P("tok", None), P(("groups", "tok"), None), P(), P(), P())
    return jax.shard_map(
        on_device, mesh=mesh, in_specs=placed, out_specs=P(("groups", "tok"), None), check_vma=False
    )
```

profile of v0, /device:TPU:0, one launch (start us, length us, event | category | flops | bytes accessed | tf_op | source)
XLA Modules:
  0.0 361.4 jit_solution(7146181306286571714)
XLA Ops:
  11.8 3.8 %convolution_convert_fusion = bf16[1024,1024]{1,0:T(8,128)(2,1)} fusion(bf16[1024,1024]{1,0:T(8,128)(2,1)S(1)} %copy-done, bf16[1024,1024]{1,0:T(8,128)(2,1)S(1)} %copy-done.1, f32[1024]{0:T(1024)S(1)} %add_rsqrt_fusion, f32[1024]{0:T(1024)S(1)} %broadcast_multiply_fusion), kind=kOutput, calls=%fused_computation.21 | convolution fusion | flops 2152726528 | bytes 6299648 | tf_op jit(solution)/shard_map/dot_general | solution.py:42
  15.6 3.8 %convolution_convert_fusion.1 = bf16[1024,1024]{1,0:T(8,128)(2,1)} fusion(bf16[1024,1024]{1,0:T(8,128)(2,1)S(1)} %copy-done.2, bf16[1024,1024]{1,0:T(8,128)(2,1)S(1)} %copy-done.1, f32[1024]{0:T(1024)S(1)} %add_rsqrt_fusion, f32[1024]{0:T(1024)S(1)} %broadcast_multiply_fusion), kind=kOutput, calls=%fused_computation.22 | convolution fusion | flops 2152726528 | bytes 6299648 | tf_op jit(solution)/shard_map/dot_general | solution.py:41
  19.4 34.3 %all-gather.2.cloned.1.call-done = bf16[1024,1024]{1,0:T(8,128)(2,1)} async-done(((bf16[64,1024]{1,0:T(8,128)(2,1)}), bf16[1024,1024]{1,0:T(8,128)(2,1)}) %all-gather.2.cloned.1.call-update) | async-done | bytes 2097168 | tf_op jit(solution)/shard_map/all_gather | solution.py:39
  53.7 107.7 %while.14 = (s32[]{:T(128)}, f32[16,1024]{1,0:T(8,128)S(1)}, f32[16,1024]{1,0:T(8,128)S(1)}, f32[16,1024,64]{1,2,0:T(8,128)}, s32[16]{0:T(128)S(1)}, /*index=5*/...) while((s32[]{:T(128)}, f32[16,1024]{1,0:T(8,128)S(1)}, ...), condition=%wide.region_5.6_spmd, body=%wide.region_2.5_spmd.sunk | while | flops 276822016 | bytes 13665979 | solution.py:49
  63.5 2.6 fusion.37
  70.3 2.6 fusion.37
  77.0 2.6 fusion.37
  83.7 2.6 fusion.37
  90.5 2.6 fusion.37
  97.2 2.6 fusion.37
  103.9 2.6 fusion.37
  110.7 2.6 fusion.37
  117.4 2.6 fusion.37
  124.1 2.6 fusion.37
  130.9 2.6 fusion.37
  137.6 2.6 fusion.37
  144.3 2.6 fusion.37
  157.8 2.6 fusion.37
  161.3 59.5 %pmax.7 = bf16[1024,16]{0,1:T(8,128)(2,1)S(1)} all-reduce(bf16[1024,16]{0,1:T(8,128)(2,1)S(1)} %bitcast_convert_fusion), channel_id=1, replica_groups=mesh['groups'=2,'tok'=16] {'tok'}, use_global_device_ids=true, to_apply=%region_6.7 | all-reduce | flops 16384 | bytes 65536 | tf_op jit(solution)/shard_map/pmax | solution.py:55
  222.0 5.1 %bitcast_multiply_fusion = f32[1024,16,64]{0,2,1:T(8,128)} fusion(f32[16,1024,64]{1,2,0:T(8,128)} %get-tuple-element.49, f32[1024,16]{0,1:T(8,128)S(1)} %get-tuple-element.69), kind=kLoop, calls=%fused_computation.20 | loop fusion | flops 1048576 | bytes 8454144 | tf_op jit(solution)/shard_map/mul | solution.py:57
  227.0 5.4 %copy.6 = f32[1024,1024]{1,0:T(8,128)} copy(f32[1024,1024]{0,1:T(8,128)} %bitcast.36) | data formatting | bytes 8388608
  232.5 42.6 %reduce-scatter.9.cloned.1.call-done = f32[64,16]{1,0:T(8,128)} async-done(((f32[1024,16]{1,0:T(8,128)}), f32[64,16]{1,0:T(8,128)}) %reduce-scatter.9.cloned.1.call-update) | async-done | bytes 4112
  275.9 75.0 %reduce-scatter.7.cloned.1.call-done = f32[64,1024]{1,0:T(8,128)} async-done(((f32[1024,1024]{1,0:T(8,128)}), f32[64,1024]{1,0:T(8,128)}) %reduce-scatter.7.cloned.1.call-update) | async-done | bytes 262160
  352.1 2.8 convolution_convert_fusion.2
  (108 shorter events, 68.3 us)
Async XLA Ops:
  6.5 5.2 %copy-start = (bf16[1024,1024]{1,0:T(8,128)(2,1)S(1)}, bf16[1024,1024]{1,0:T(8,128)(2,1)}, u32[]{:S(2)}) copy-start(bf16[1024,1024]{1,0:T(8,128)(2,1)} %param.10) | copy-start | bytes 6291460
  6.5 47.1 %all-gather.2.cloned.1.call-start = ((), (), s32[]{:S(2)}) async-start(), calls=%async_computation.2 | async-start | bytes 2228224 | tf_op jit(solution)/shard_map/all_gather | solution.py:39
  7.3 267.8 %reduce-scatter.9.cloned.1.call-start = ((), (), s32[]{:S(2)}) async-start(), calls=%async_computation.4 | async-start | bytes 557056
  7.3 4.4 %copy-start.1 = (bf16[1024,1024]{1,0:T(8,128)(2,1)S(1)}, bf16[1024,1024]{1,0:T(8,128)(2,1)}, u32[]{:S(2)}) copy-start(bf16[1024,1024]{1,0:T(8,128)(2,1)} %param.8) | copy-start | bytes 6291460
  11.8 3.8 %copy-start.2 = (bf16[1024,1024]{1,0:T(8,128)(2,1)S(1)}, bf16[1024,1024]{1,0:T(8,128)(2,1)}, u32[]{:S(2)}) copy-start(bf16[1024,1024]{1,0:T(8,128)(2,1)} %param.9) | copy-start | bytes 6291460
  221.9 129.0 %reduce-scatter.7.cloned.1.call-start = ((), (), s32[]{:S(2)}) async-start(), calls=%async_computation.3 | async-start | bytes 4456448
Sparse Core Ops, SparseCore 0:
  9.5 44.0 all-gather.1
  222.1 52.9 reduce-scatter.8
  279.4 71.4 reduce-scatter.6
where the time goes:
time: 363 us; the launch traced here: 361 us
  waiting for transfers between devices  153 us (42%)
  matrix products  81 us (22%)
  blocking collectives  59.5 us (16%)
  local copies, waits for them, and re-layouts  22.2 us (6%)
  other arithmetic  21.2 us (6%)
  between operations  13.2 us (4%)
  loops' own time  11.5 us (3%)
    unnamed x5, waiting for transfers between devices  118 us
    pmax x1, blocking collectives, on_device(): lax.pmax(row_max.astype(jnp.bfloat16), 'tok').astype(row_max.dtype)  59.5 us
    dot_general x16, matrix products, head_partials(): jnp.dot(weights.astype(jnp.bfloat16), head_values, preferred_element_type...  41.3 us
    all_gather x1, waiting for transfers between devices, on_device(): gathered = lax.all_gather(queries, 'tok', axis=0, tiled=True)  34.3 us
    dot_general x16, matrix products, head_partials(): lax.dot_general(head_query, head_keys, (((1,), (1,)), ((), ())), preferre...  29.4 us
    reduce_sum x16, other arithmetic, head_partials(): totals = jnp.sum(weights, axis=1)  11.7 us
    another operation x1, loops' own time, on_device(): lax.map(one_head, jnp.arange(H, dtype=jnp.int32))  11.5 us
    dynamic_slice x16, local copies, waits for them, and re-layouts, on_device(): lax.map(one_head, jnp.arange(H, dtype=jnp.int32))  10.4 us
  transfers between devices with their start and end apart: 3, of which 3 were waited for; matrix products, arithmetic and copies ran while one was open for 6% of the time, Pallas kernels for 0%

commit v1 on v0

--- a/solution.py
+++ b/solution.py
@@ -1,6 +1,11 @@
+import functools
+import math
+
 import jax
 import jax.numpy as jnp
 from jax import lax
+from jax.experimental import pallas as pl
+from jax.experimental.pallas import tpu as pltpu
 from jax.sharding import PartitionSpec as P
 
 H = 16
@@ -68,8 +73,221 @@
     return jnp.dot(attended, out_weight, preferred_element_type=jnp.float32).astype(jnp.bfloat16)
 
 
+GROUPS = 4
+GH = H // GROUPS
+GC = GH * HD
+PAIRS = H // 2
+GP = GH // 2
+CHUNKS = 4
+EXPO = math.log2(math.e) * HD ** (-0.5)
+
+
+def fused(n, q_in, x_ref, wk_ref, wv_ref, wo_ref, out_ref,
+          q_ref, k_ref, v_ref, acc_ref, st_ref, sbuf, rbuf, rst,
+          att_ref, qs_sem, qr_sem, os_sem, or_sem, ts_sem, tr_sem):
+    steps = n.bit_length() - 1
+    rows = q_in.shape[0]
+    tokens = x_ref.shape[0]
+    me = lax.axis_index("tok")
+    bits = [n >> (s + 1) for s in range(steps)]
+
+    def partner(bit):
+        return me + bit - 2 * bit * lax.rem(me // bit, 2)
+
+    barrier = pltpu.get_barrier_semaphore()
+    for bit in bits:
+        pl.semaphore_signal(barrier, inc=1, device_id={"tok": partner(bit)}, device_id_type=pl.DeviceIdType.MESH)
+    pl.semaphore_wait(barrier, steps)
+
+    def gather(s):
+        have = 1 << s
+        return pltpu.make_async_remote_copy(
+            src_ref=q_ref.at[pl.ds(0, have)], dst_ref=q_ref.at[pl.ds(have, have)],
+            send_sem=qs_sem.at[s], recv_sem=qr_sem.at[s],
+            device_id={"tok": partner(n >> (s + 1))}, device_id_type=pl.DeviceIdType.MESH)
+
+    def reduce_out(g, s):
+        half = n >> (s + 1)
+        return pltpu.make_async_remote_copy(
+            src_ref=sbuf.at[g, pl.ds(half, half)], dst_ref=rbuf.at[g, pl.ds(half, half)],
+            send_sem=os_sem.at[g, s], recv_sem=or_sem.at[g, s],
+            device_id={"tok": partner(1 << s)}, device_id_type=pl.DeviceIdType.MESH)
+
+    def reduce_stat(g, s):
+        half = n >> (s + 1)
+        return pltpu.make_async_remote_copy(
+            src_ref=st_ref.at[g, pl.ds(half, half)], dst_ref=rst.at[g, pl.ds(half, half)],
+            send_sem=ts_sem.at[g, s], recv_sem=tr_sem.at[g, s],
+            device_id={"tok": partner(1 << s)}, device_id_type=pl.DeviceIdType.MESH)
+
+    q_ref[0] = q_in[...]
+    gather(0).start()
+
+    part = tokens // CHUNKS
+
+    def project(c):
+        first = c * part
+        x = x_ref[pl.ds(first, part), :].astype(jnp.float32)
+        center = x - jnp.mean(x, axis=1, keepdims=True)
+        spread = jnp.mean(center * center, axis=1, keepdims=True)
+        normed = (center * lax.rsqrt(spread + epsilon)).astype(jnp.bfloat16)
+        ones = jnp.ones((part, 2 * HD), jnp.bfloat16)
+        keys = jnp.dot(normed, wk_ref[...], preferred_element_type=jnp.float32).astype(jnp.bfloat16)
+        for p in range(PAIRS):
+            k_ref[p, pl.ds(first, part), :] = keys[:, p * 128 : (p + 1) * 128]
+        values = jnp.dot(normed, wv_ref[...], preferred_element_type=jnp.float32).astype(jnp.bfloat16)
+        for p in range(PAIRS):
+            v_ref[p, pl.ds(first, part), 0:128] = values[:, p * 128 : (p + 1) * 128]
+            v_ref[p, pl.ds(first, part), 128:256] = ones
+
+    def project_some(first, last):
+        @pl.loop(first, last)
+        def _(c):
+            project(c)
+
+    project_some(0, CHUNKS // 2)
+    gather(0).wait_recv()
+    gather(1).start()
+    project_some(CHUNKS // 2, CHUNKS)
+    gather(1).wait_recv()
+    gather(2).start()
+
+    quarter = n // 4
+    chunk = quarter * rows
+    lane = lax.broadcasted_iota(jnp.int32, (chunk, 128), 1)
+
+    def attend(g, q):
+        stats = jnp.zeros((chunk, 128), jnp.float32)
+        for j in range(GP):
+            pair = g * GP + j
+            cols = pl.ds(pl.multiple_of(pair * 128, 128), 128)
+            query = q_ref[pl.ds(q * quarter, quarter), :, cols].reshape(chunk, 128)
+            zero = jnp.zeros_like(query)
+            both = jnp.concatenate([jnp.where(lane < HD, query, zero), jnp.where(lane < HD, zero, query)], axis=0)
+            scores = lax.dot_general(both, k_ref[pair], (((1,), (1,)), ((), ())), preferred_element_type=jnp.float32)
+            top = jnp.max(scores, axis=1, keepdims=True)
+            weights = jnp.exp2((scores - top) * EXPO).astype(jnp.bfloat16)
+            product = jnp.dot(weights, v_ref[pair], preferred_element_type=jnp.float32)
+            merged = jnp.where(lane < HD, product[:chunk, :128], product[chunk:, :128]).reshape(quarter, rows, 128)
+            where = slice(j * 128, (j + 1) * 128)
+            if q < 2:
+                acc_ref[g, pl.ds(q * quarter, quarter), :, where] = merged
+            else:
+                sbuf[g, pl.ds(q * quarter, quarter), :, where] = merged.astype(jnp.bfloat16)
+            for e in range(2):
+                mine = slice(e * chunk, (e + 1) * chunk)
+                stats = jnp.where(lane == 2 * j + e, top[mine], stats)
+                stats = jnp.where(lane == GH + 2 * j + e, product[mine, 128:], stats)
+        for b in range(quarter):
+            turned = stats[b * rows : (b + 1) * rows].T
+            st_ref[g, q * quarter + b] = turned[: 2 * GH]
+
+    narrow = lax.broadcasted_iota(jnp.int32, (rows, 128), 1) < HD
+
+    def spread_heads(turned):
+        return jnp.concatenate(
+            [jnp.where(narrow, turned[:, 2 * j : 2 * j + 1], turned[:, 2 * j + 1 : 2 * j + 2]) for j in range(GP)], axis=1)
+
+    def combine(g, s):
+        half = n >> (s + 1)
+        reduce_out(g, s).wait_recv()
+        reduce_stat(g, s).wait_recv()
+
+        def one(b):
+            own, other = st_ref[g, b], rst[g, half + b]
+            top = jnp.maximum(own[:GH], other[:GH])
+            f_own = jnp.exp2((own[:GH] - top) * EXPO)
+            f_other = jnp.exp2((other[:GH] - top) * EXPO)
+            total = own[GH:] * f_own + other[GH:] * f_other
+            st_ref[g, b] = jnp.concatenate([top, total], axis=0)
+            turned = jnp.concatenate([f_own, f_other], axis=0).T
+            summed = (acc_ref[g, b] * spread_heads(turned[:, :GH])
+                      + rbuf[g, half + b].astype(jnp.float32) * spread_heads(turned[:, GH:]))
+            return summed
+
+        for b in range(half):
+            summed = one(b)
+            if b >= half // 2 and half > 1:
+                sbuf[g, b] = summed.astype(jnp.bfloat16)
+            else:
+                acc_ref[g, b] = summed
+        if s + 1 < steps:
+            reduce_out(g, s + 1).start()
+            reduce_stat(g, s + 1).start()
+
+    @pl.loop(0, GROUPS)
+    def _(g):
+        for q in range(4):
+            if q in (1, 2):
+                @pl.when(g == 0)
+                def _():
+                    gather(q + 1).wait_recv()
+                    if q + 2 < steps:
+                        gather(q + 2).start()
+            attend(g, q)
+            if q == 3:
+                reduce_out(g, 0).start()
+                reduce_stat(g, 0).start()
+
+            @pl.when(g > 0)
+            def _():
+                combine(g - 1, q)
+
+    for s in range(steps):
+        combine(GROUPS - 1, s)
+
+    for g in range(GROUPS):
+        share = spread_heads(st_ref[g, 0].T[:, GH:])
+        att_ref[:, g * GC : (g + 1) * GC] = (acc_ref[g, 0] / share).astype(jnp.bfloat16)
+    out_ref[...] = jnp.dot(att_ref[...], wo_ref[...], preferred_element_type=jnp.float32).astype(out_ref.dtype)
+
+    for s in range(steps):
+        gather(s).wait_send()
+
+    @pl.loop(0, GROUPS)
+    def _(g):
+        for s in range(steps):
+            reduce_out(g, s).wait_send()
+            reduce_stat(g, s).wait_send()
+
+
+def program(queries, tokens, key_weight, value_weight, out_weight):
+    n = lax.axis_size("tok")
+    rows, width = queries.shape
+    count = tokens.shape[0]
+    if n != 16 or rows % 16 or count % 1024 or width != H * HD:
+        return on_device(queries, tokens, key_weight, value_weight, out_weight)
+    vmem = pl.BlockSpec(memory_space=pltpu.VMEM)
+    steps = n.bit_length() - 1
+    return pl.pallas_call(
+        functools.partial(fused, n),
+        out_shape=jax.ShapeDtypeStruct((rows, width), jnp.bfloat16),
+        in_specs=[vmem] * 5,
+        out_specs=vmem,
+        scratch_shapes=[
+            pltpu.VMEM((n, rows, width), jnp.bfloat16),
+            pltpu.VMEM((PAIRS, count, 128), jnp.bfloat16),
+            pltpu.VMEM((PAIRS, count, 256), jnp.bfloat16),
+            pltpu.VMEM((GROUPS, n // 2, rows, GC), jnp.float32),
+            pltpu.VMEM((GROUPS, n, 2 * GH, rows), jnp.float32),
+            pltpu.VMEM((GROUPS, n, rows, GC), jnp.bfloat16),
+            pltpu.VMEM((GROUPS, n, rows, GC), jnp.bfloat16),
+            pltpu.VMEM((GROUPS, n, 2 * GH, rows), jnp.float32),
+            pltpu.VMEM((rows, width), jnp.bfloat16),
+            pltpu.SemaphoreType.DMA((steps,)),
+            pltpu.SemaphoreType.DMA((steps,)),
+            pltpu.SemaphoreType.DMA((GROUPS, steps)),
+            pltpu.SemaphoreType.DMA((GROUPS, steps)),
+            pltpu.SemaphoreType.DMA((GROUPS, steps)),
+            pltpu.SemaphoreType.DMA((GROUPS, steps)),
+        ],
+        compiler_params=pltpu.CompilerParams(
+            collective_id=0, has_side_effects=True, vmem_limit_bytes=56 * 2**20),
+    )(queries, tokens, key_weight, value_weight, out_weight)
+
+
 def solution(mesh):
     placed = (P("tok", None), P(("groups", "tok"), None), P(), P(), P())
     return jax.shard_map(
-        on_device, mesh=mesh, in_specs=placed, out_specs=P(("groups", "tok"), None), check_vma=False
-    )
+        program, mesh=mesh, in_specs=placed, out_specs=P(("groups", "tok"), None), check_vma=False
+    )

time: 363 us -> 106 us (0.29)
  waiting for transfers between devices: 153 us -> 0 us
  Pallas kernels: 0 us -> 104 us
  matrix products: 81 us -> 0 us
  blocking collectives: 59.5 us -> 0 us
  other arithmetic: 21.2 us -> 0 us
  local copies, waits for them, and re-layouts: 22.2 us -> 1.57 us
  between operations: 13.2 us -> 0.01 us
  loops' own time: 11.5 us -> 0 us
    unnamed x5 -> x0, waiting for transfers between devices: 118 us -> none
    pallas_call x0 -> x1, Pallas kernels: none -> 104 us  [program(): pl.pallas_call(functools.partial(fused, n), out_shape=jax.ShapeDtypeStruc...]
    dot_general x35 -> x0, matrix products: 81 us -> none  [the longest x16 41.3 us: head_partials(): jnp.dot(weights.astype(jnp.bfloat16), head_values, preferred_element_type...]
    pmax x1 -> x0, blocking collectives: 59.5 us -> none  [on_device(): lax.pmax(row_max.astype(jnp.bfloat16), 'tok').astype(row_max.dtype)]
    all_gather x1 -> x0, waiting for transfers between devices: 34.3 us -> none  [on_device(): gathered = lax.all_gather(queries, 'tok', axis=0, tiled=True)]
    reduce_sum x18 -> x0, other arithmetic: 16.1 us -> none  [the longest x16 11.7 us: head_partials(): totals = jnp.sum(weights, axis=1)]
    another operation x1 -> x0, loops' own time: 11.5 us -> none  [on_device(): lax.map(one_head, jnp.arange(H, dtype=jnp.int32))]
    dynamic_slice x16 -> x0, local copies, waits for them, and re-layouts: 10.4 us -> none  [on_device(): lax.map(one_head, jnp.arange(H, dtype=jnp.int32))]
  transfers between devices with their start and end apart: 3 -> 0, of which waited for: 3 -> 0; matrix products, arithmetic and copies ran while one was open for 6% -> 0% of each run, Pallas kernels for 0% -> 0%
where the time goes in v1:
time: 106 us
  Pallas kernels  104 us (98%)
  local copies, waits for them, and re-layouts  1.57 us (1%)
    pallas_call x1, Pallas kernels, program(): pl.pallas_call(functools.partial(fused, n), out_shape=jax.ShapeDtypeStruc...  104 us

profile of v1, /device:TPU:0, one launch (start us, length us, event | category | flops | bytes accessed | tf_op | source)
XLA Modules:
  0.0 105.7 jit_solution(16178779309285079798)
XLA Ops:
  0.0 104.1 %shard_map.55 = bf16[64,1024]{1,0:T(8,128)(2,1)} custom-call(bf16[64,1024]{1,0:T(8,128)(2,1)} %q_in.1, bf16[1024,1024]{1,0:T(8,128)(2,1)} %x_ref.1, bf16[1024,1024]{1,0:T(8,128)(2,1)} %wk_ref.1, bf16[1024,1024]{1,0:T(8,128)(2,1)} %wv_ref.1, bf16[1024,1024]{1,0:T(8,128)(2,1)} %wo_ref.1), custom_call_target="tpu_custom_call" | custom-call | tf_op jit(solution)/shard_map/pallas_call | solution.py:262
  104.1 1.6 %copy.7 = bf16[64,1024]{1,0:T(8,128)(2,1)} copy(bf16[64,1024]{1,0:T(8,128)(2,1)} %shard_map.55) | data formatting | bytes 262144

commit v2 on v1

--- a/solution.py
+++ b/solution.py
@@ -82,7 +82,8 @@
 EXPO = math.log2(math.e) * HD ** (-0.5)
 
 
-def fused(n, q_in, x_ref, wk_ref, wv_ref, wo_ref, out_ref,
+def fused(n, q_in, x_in, wk_in, wv_in, wo_in, out_ref,
+          x_ref, wk_ref, wv_ref, wo_ref, load_sem,
           q_ref, k_ref, v_ref, acc_ref, st_ref, sbuf, rbuf, rst,
           att_ref, qs_sem, qr_sem, os_sem, or_sem, ts_sem, tr_sem):
     steps = n.bit_length() - 1
@@ -94,9 +95,15 @@
     def partner(bit):
         return me + bit - 2 * bit * lax.rem(me // bit, 2)
 
+    loads = [
+        pltpu.make_async_copy(src, dst, load_sem.at[i])
+        for i, (src, dst) in enumerate(((x_in, x_ref), (wk_in, wk_ref), (wv_in, wv_ref), (wo_in, wo_ref)))]
     barrier = pltpu.get_barrier_semaphore()
     for bit in bits:
         pl.semaphore_signal(barrier, inc=1, device_id={"tok": partner(bit)}, device_id_type=pl.DeviceIdType.MESH)
+    for load in loads:
+        load.start()
+    q_ref[0] = q_in[...]
     pl.semaphore_wait(barrier, steps)
 
     def gather(s):
@@ -120,7 +127,6 @@
             send_sem=ts_sem.at[g, s], recv_sem=tr_sem.at[g, s],
             device_id={"tok": partner(1 << s)}, device_id_type=pl.DeviceIdType.MESH)
 
-    q_ref[0] = q_in[...]
     gather(0).start()
 
     part = tokens // CHUNKS
@@ -145,6 +151,8 @@
         def _(c):
             project(c)
 
+    for load in loads[:3]:
+        load.wait()
     project_some(0, CHUNKS // 2)
     gather(0).wait_recv()
     gather(1).start()
@@ -217,28 +225,37 @@
 
     @pl.loop(0, GROUPS)
     def _(g):
-        for q in range(4):
-            if q in (1, 2):
-                @pl.when(g == 0)
-                def _():
-                    gather(q + 1).wait_recv()
-                    if q + 2 < steps:
-                        gather(q + 2).start()
-            attend(g, q)
-            if q == 3:
-                reduce_out(g, 0).start()
-                reduce_stat(g, 0).start()
-
-            @pl.when(g > 0)
+        attend(g, 0)
+
+    gather(2).wait_recv()
+    gather(3).start()
+
+    @pl.loop(0, GROUPS)
+    def _(g):
+        attend(g, 1)
+
+    gather(3).wait_recv()
+
+    @pl.loop(0, GROUPS)
+    def _(g):
+        attend(g, 2)
+        attend(g, 3)
+        reduce_out(g, 0).start()
+        reduce_stat(g, 0).start()
+        for s in reversed(range(min(steps, GROUPS - 1))):
+            @pl.when(g > s)
             def _():
-                combine(g - 1, q)
-
-    for s in range(steps):
-        combine(GROUPS - 1, s)
+                combine(g - 1 - s, s)
+
+    for t in range(GROUPS, GROUPS + steps):
+        for s in reversed(range(steps)):
+            if 0 <= t - 1 - s < GROUPS:
+                combine(t - 1 - s, s)
 
     for g in range(GROUPS):
         share = spread_heads(st_ref[g, 0].T[:, GH:])
         att_ref[:, g * GC : (g + 1) * GC] = (acc_ref[g, 0] / share).astype(jnp.bfloat16)
+    loads[3].wait()
     out_ref[...] = jnp.dot(att_ref[...], wo_ref[...], preferred_element_type=jnp.float32).astype(out_ref.dtype)
 
     for s in range(steps):
@@ -262,9 +279,14 @@
     return pl.pallas_call(
         functools.partial(fused, n),
         out_shape=jax.ShapeDtypeStruct((rows, width), jnp.bfloat16),
-        in_specs=[vmem] * 5,
+        in_specs=[vmem] + [pl.BlockSpec(memory_space=pl.ANY)] * 4,
         out_specs=vmem,
         scratch_shapes=[
+            pltpu.VMEM(tokens.shape, tokens.dtype),
+            pltpu.VMEM(key_weight.shape, key_weight.dtype),
+            pltpu.VMEM(value_weight.shape, value_weight.dtype),
+            pltpu.VMEM(out_weight.shape, out_weight.dtype),
+            pltpu.SemaphoreType.DMA((4,)),
             pltpu.VMEM((n, rows, width), jnp.bfloat16),
             pltpu.VMEM((PAIRS, count, 128), jnp.bfloat16),
             pltpu.VMEM((PAIRS, count, 256), jnp.bfloat16),

time: 106 us -> 79.5 us (0.75)
  Pallas kernels: 104 us -> 77.8 us
    pallas_call x1, Pallas kernels: 104 us -> 77.8 us  [program(): pl.pallas_call(functools.partial(fused, n), out_shape=jax.ShapeDtypeStruc...]
where the time goes in v2:
time: 79.5 us; the launch traced here: 79.3 us
  Pallas kernels  77.8 us (98%)
  local copies, waits for them, and re-layouts  1.57 us (2%)
    pallas_call x1, Pallas kernels, program(): pl.pallas_call(functools.partial(fused, n), out_shape=jax.ShapeDtypeStruc...  77.8 us

profile of v2, /device:TPU:0, one launch (start us, length us, event | category | flops | bytes accessed | tf_op | source)
XLA Modules:
  0.0 79.3 jit_solution(14317204006524745228)
XLA Ops:
  0.0 77.8 %shard_map.55 = bf16[64,1024]{1,0:T(8,128)(2,1)} custom-call(bf16[64,1024]{1,0:T(8,128)(2,1)} %q_in.1, bf16[1024,1024]{1,0:T(8,128)(2,1)} %x_in.1, bf16[1024,1024]{1,0:T(8,128)(2,1)} %wk_in.1, bf16[1024,1024]{1,0:T(8,128)(2,1)} %wv_in.1, bf16[1024,1024]{1,0:T(8,128)(2,1)} %wo_in.1), custom_call_target="tpu_custom_call" | custom-call | tf_op jit(solution)/shard_map/pallas_call | solution.py:279
  77.8 1.6 %copy.7 = bf16[64,1024]{1,0:T(8,128)(2,1)} copy(bf16[64,1024]{1,0:T(8,128)(2,1)} %shard_map.55) | data formatting | bytes 262144

commit v3 on v2

--- a/solution.py
+++ b/solution.py
@@ -106,12 +106,19 @@
     q_ref[0] = q_in[...]
     pl.semaphore_wait(barrier, steps)
 
-    def gather(s):
-        have = 1 << s
+    def gather(s, part):
+        first = 0 if part == 0 else 1 << (part - 1)
+        size = max(first, 1)
         return pltpu.make_async_remote_copy(
-            src_ref=q_ref.at[pl.ds(0, have)], dst_ref=q_ref.at[pl.ds(have, have)],
-            send_sem=qs_sem.at[s], recv_sem=qr_sem.at[s],
+            src_ref=q_ref.at[pl.ds(first, size)], dst_ref=q_ref.at[pl.ds((1 << s) + first, size)],
+            send_sem=qs_sem.at[s, part], recv_sem=qr_sem.at[s, part],
             device_id={"tok": partner(n >> (s + 1))}, device_id_type=pl.DeviceIdType.MESH)
+
+    def arrived(k):
+        for part in range(k + 1):
+            gather(k, part).wait_recv()
+        for s in range(k + 1, steps):
+            gather(s, k + 1).start()
 
     def reduce_out(g, s):
         half = n >> (s + 1)
@@ -127,7 +134,8 @@
             send_sem=ts_sem.at[g, s], recv_sem=tr_sem.at[g, s],
             device_id={"tok": partner(1 << s)}, device_id_type=pl.DeviceIdType.MESH)
 
-    gather(0).start()
+    for s in range(steps):
+        gather(s, 0).start()
 
     part = tokens // CHUNKS
 
@@ -153,12 +161,10 @@
 
     for load in loads[:3]:
         load.wait()
-    project_some(0, CHUNKS // 2)
-    gather(0).wait_recv()
-    gather(1).start()
-    project_some(CHUNKS // 2, CHUNKS)
-    gather(1).wait_recv()
-    gather(2).start()
+    project_some(0, CHUNKS - 1)
+    arrived(0)
+    project_some(CHUNKS - 1, CHUNKS)
+    arrived(1)
 
     quarter = n // 4
     chunk = quarter * rows
@@ -227,14 +233,13 @@
     def _(g):
         attend(g, 0)
 
-    gather(2).wait_recv()
-    gather(3).start()
-
-    @pl.loop(0, GROUPS)
+    arrived(2)
+
+    @pl.loop(0, GROUPS - 1)
     def _(g):
         attend(g, 1)
 
-    gather(3).wait_recv()
+    arrived(3)
 
     @pl.loop(0, GROUPS)
     def _(g):
@@ -247,6 +252,7 @@
             def _():
                 combine(g - 1 - s, s)
 
+    attend(GROUPS - 1, 1)
     for t in range(GROUPS, GROUPS + steps):
         for s in reversed(range(steps)):
             if 0 <= t - 1 - s < GROUPS:
@@ -259,7 +265,8 @@
     out_ref[...] = jnp.dot(att_ref[...], wo_ref[...], preferred_element_type=jnp.float32).astype(out_ref.dtype)
 
     for s in range(steps):
-        gather(s).wait_send()
+        for part in range(s + 1):
+            gather(s, part).wait_send()
 
     @pl.loop(0, GROUPS)
     def _(g):
@@ -296,8 +303,8 @@
             pltpu.VMEM((GROUPS, n, rows, GC), jnp.bfloat16),
             pltpu.VMEM((GROUPS, n, 2 * GH, rows), jnp.float32),
             pltpu.VMEM((rows, width), jnp.bfloat16),
-            pltpu.SemaphoreType.DMA((steps,)),
-            pltpu.SemaphoreType.DMA((steps,)),
+            pltpu.SemaphoreType.DMA((steps, steps)),
+            pltpu.SemaphoreType.DMA((steps, steps)),
             pltpu.SemaphoreType.DMA((GROUPS, steps)),
             pltpu.SemaphoreType.DMA((GROUPS, steps)),
             pltpu.SemaphoreType.DMA((GROUPS, steps)),

time: 79.5 us -> 70.9 us (0.89)
  Pallas kernels: 77.8 us -> 69.2 us
    pallas_call x1, Pallas kernels: 77.8 us -> 69.2 us  [program(): pl.pallas_call(functools.partial(fused, n), out_shape=jax.ShapeDtypeStruc...]
where the time goes in v3:
time: 70.9 us; the launch traced here: 70.7 us
  Pallas kernels  69.2 us (98%)
  local copies, waits for them, and re-layouts  1.57 us (2%)
    pallas_call x1, Pallas kernels, program(): pl.pallas_call(functools.partial(fused, n), out_shape=jax.ShapeDtypeStruc...  69.2 us
    unnamed x1, local copies, waits for them, and re-layouts  1.57 us

profile of v3, /device:TPU:0, one launch (start us, length us, event | category | flops | bytes accessed | tf_op | source)
XLA Modules:
  0.0 70.7 jit_solution(11594486425528144115)
XLA Ops:
  0.0 69.2 %shard_map.55 = bf16[64,1024]{1,0:T(8,128)(2,1)} custom-call(bf16[64,1024]{1,0:T(8,128)(2,1)} %q_in.1, bf16[1024,1024]{1,0:T(8,128)(2,1)} %x_in.1, bf16[1024,1024]{1,0:T(8,128)(2,1)} %wk_in.1, bf16[1024,1024]{1,0:T(8,128)(2,1)} %wv_in.1, bf16[1024,1024]{1,0:T(8,128)(2,1)} %wo_in.1), custom_call_target="tpu_custom_call" | custom-call | tf_op jit(solution)/shard_map/pallas_call | solution.py:286
  69.2 1.6 %copy.7 = bf16[64,1024]{1,0:T(8,128)(2,1)} copy(bf16[64,1024]{1,0:T(8,128)(2,1)} %shard_map.55) | data formatting | bytes 262144

commit v4 on v3

--- a/solution.py
+++ b/solution.py
@@ -254,7 +254,7 @@
 
     attend(GROUPS - 1, 1)
     for t in range(GROUPS, GROUPS + steps):
-        for s in reversed(range(steps)):
+        for s in range(steps):
             if 0 <= t - 1 - s < GROUPS:
                 combine(t - 1 - s, s)
 

time: 70.9 us -> 68.1 us (0.961)
  Pallas kernels: 69.2 us -> 66.4 us
    pallas_call x1, Pallas kernels: 69.2 us -> 66.4 us  [program(): pl.pallas_call(functools.partial(fused, n), out_shape=jax.ShapeDtypeStruc...]
where the time goes in v4:
time: 68.1 us; the launch traced here: 68 us
  Pallas kernels  66.4 us (98%)
  local copies, waits for them, and re-layouts  1.57 us (2%)
    pallas_call x1, Pallas kernels, program(): pl.pallas_call(functools.partial(fused, n), out_shape=jax.ShapeDtypeStruc...  66.4 us
    unnamed x1, local copies, waits for them, and re-layouts  1.57 us

profile of v4, /device:TPU:0, one launch (start us, length us, event | category | flops | bytes accessed | tf_op | source)
XLA Modules:
  0.0 68.0 jit_solution(5154521181578794813)
XLA Ops:
  0.0 66.4 %shard_map.55 = bf16[64,1024]{1,0:T(8,128)(2,1)} custom-call(bf16[64,1024]{1,0:T(8,128)(2,1)} %q_in.1, bf16[1024,1024]{1,0:T(8,128)(2,1)} %x_in.1, bf16[1024,1024]{1,0:T(8,128)(2,1)} %wk_in.1, bf16[1024,1024]{1,0:T(8,128)(2,1)} %wv_in.1, bf16[1024,1024]{1,0:T(8,128)(2,1)} %wo_in.1), custom_call_target="tpu_custom_call" | custom-call | tf_op jit(solution)/shard_map/pallas_call | solution.py:286
  66.4 1.6 %copy.7 = bf16[64,1024]{1,0:T(8,128)(2,1)} copy(bf16[64,1024]{1,0:T(8,128)(2,1)} %shard_map.55) | data formatting | bytes 262144
